TPU v7x, 32 devices: a whole 2x2x4 slice. The times are simulated.
32 devices in a mesh: tract: 2 (over y), patch: 4 (over z), band: 2 (over x), row: 2 (over core).
Axes of the slice: x: 2, y: 2, z: 4, core: 2. Of those that a mesh axis runs over, the one named last changes fastest.
Arguments:
- tiles: bfloat16 [4, 4, 32, 256, 256], P(('tract', 'band'), 'patch', None, 'row'), parts along dimension 0, may hold values from -6 to 6
- targets: int32 [4, 4, 32, 1], P(('tract', 'band'), 'patch'), parts along dimension 0, may hold values from 0 to 3; in each aligned block of 32 rows (0 to 31, 32 to 63, ..., all dimensions but the last counted through in order) at most 16 rows name the same one
- offsets: int32 [4, 4, 32, 2], P(('tract', 'band'), 'patch'), parts along dimension 0, may hold values from -4 to 4
- fractions: bfloat16 [4, 4, 32, 2], P(('tract', 'band'), 'patch'), parts along dimension 0, may hold values from 0 to 1
- kernels: bfloat16 [4, 4, 32, 2, 7], P(('tract', 'band'), 'patch'), parts along dimension 0, may hold values from 0.049804688 to 1
- weights: bfloat16 [4, 4, 32], P(('tract', 'band'), 'patch'), parts along dimension 0, may hold values from 0.25 to 4
- band_gain: float32 [2], replicated, may hold values from 0.5 to 2
Outputs:
- coadd: float32 [4, 4, 256, 256], P(('tract', 'band'), 'patch', 'row'), parts along dimension 0
- detection: float32 [8, 256, 256], P(('tract', 'patch'), ('row', 'band')), parts along dimension 0
- difference: bfloat16 [4, 4, 32, 256, 256], P(('tract', 'band'), 'patch', None, 'row'), parts along dimension 0
There are 2 independent parts, one for each index of `tract`. A program takes and returns all parts, laid end to end along the dimension named above; an argument that names none is the same for every part. Nothing has to cross between parts.
Inputs may be any that keep to these rules, and one draw needn't show every extreme that they name: `targets`: among the 32 tiles of one device, at most 16 name the same patch, a bound that some block reaches of them.
All inputs are finite; a program needn't handle non-finite values.
Results may differ from a plain program's by a relative error of at most 0.013.
Values may be sent and summed in bfloat16 or wider, within the bound.
A program may use at most 128 MiB of HBM per device.

v0:
```python
import jax
import jax.numpy as jnp
from jax import lax
from jax.sharding import PartitionSpec as P

HALO = 12


reach = 11


def with_halo(block, sides, width):
    for axis, dim in sides:
        count = lax.axis_size(axis)
        forward = [(i, i + 1) for i in range(count - 1)]
        backward = [(target, source) for source, target in forward]
        low = lax.ppermute(
            lax.slice_in_dim(block, block.shape[dim] - width, None, axis=dim), axis, forward
        )
        high = lax.ppermute(lax.slice_in_dim(block, 0, width, axis=dim), axis, backward)
        block = jnp.concatenate([low, block, high], axis=dim)
    return block


def lanczos(value):
    return jnp.where(jnp.abs(value) < 3.0, jnp.sinc(value) * jnp.sinc(value / 3.0), 0.0)


def band_weights(rows, shifts, kernel_taps, extent):
    lag_values = jnp.arange(-reach - 3, reach + 4).astype(jnp.float32)
    lanczos_table = lanczos(lag_values[None, :] - shifts[:, None])
    result = jnp.zeros((shifts.shape[0], rows.shape[0], 2 * reach + 1), jnp.float32)
    for number in range(7):
        offset = number - 3
        inside = ((rows + offset >= 0) & (rows + offset < extent)).astype(jnp.float32)
        scaled = kernel_taps[:, number][:, None] * inside[None, :]
        result = (
            result
            + scaled[:, :, None] * lanczos_table[:, None, 3 - offset : 3 - offset + 2 * reach + 1]
        )
    return result


def spread(band, rows, columns):
    lagged = columns[None, :] - rows[:, None]
    result = jnp.zeros((band.shape[0], rows.shape[0], columns.shape[0]), jnp.float32)
    for number in range(2 * reach + 1):
        result = result + jnp.where(
            (lagged == number - reach)[None], band[:, :, number : number + 1], 0.0
        )
    return result


def column_operator(params, extent):
    values = params.astype(jnp.float32)
    rows = jnp.arange(extent)
    band = band_weights(rows, values[:, 0] + values[:, 2], values[:, 4:11], extent)
    return spread(band, rows, rows).astype(jnp.bfloat16)


def warp_rows(images, params, col_op, first_row, extent):
    values = params.astype(jnp.float32)
    height = images.shape[1]
    section = jnp.einsum("nrj,nij->nri", images, col_op, preferred_element_type=jnp.float32).astype(
        jnp.bfloat16
    )
    extended = with_halo(section, (("row", 1),), HALO)
    mine = first_row + jnp.arange(height)
    beside_all = first_row - HALO + jnp.arange(height + 2 * HALO)
    band = band_weights(mine, values[:, 1] + values[:, 3], values[:, 11:18], extent)
    row_op = spread(band, mine, beside_all).astype(jnp.bfloat16)
    return jnp.einsum("nim,nmc->nic", row_op, extended, preferred_element_type=jnp.float32).astype(
        jnp.bfloat16
    )


def back_project(extended, params, col_op, first_row, extent):
    values = params.astype(jnp.float32)
    height = extended.shape[-2] - 2 * HALO
    mine = first_row + jnp.arange(height)
    beside_all = first_row - HALO + jnp.arange(height + 2 * HALO)
    band = band_weights(beside_all, values[:, 1] + values[:, 3], values[:, 11:18], extent)
    row_op = spread(band, beside_all, mine).astype(jnp.bfloat16)
    partial_back = jnp.einsum("nij,ic->njc", row_op, extended, preferred_element_type=jnp.float32)
    partial_back = partial_back.astype(jnp.bfloat16)
    return jnp.einsum(
        "nji,nic->njc", partial_back, col_op, preferred_element_type=jnp.float32
    ).astype(jnp.bfloat16)


def source_sums(warped, slot_weight, peers, depth):
    flat = warped.reshape(peers, depth, -1)
    grouped = jnp.einsum(
        "sd,sdx->sx", slot_weight.reshape(peers, depth), flat, preferred_element_type=jnp.float32
    )
    return jnp.sum(grouped.astype(jnp.bfloat16).astype(jnp.float32), axis=0)


def body(tiles, targets, offsets, fractions, kernels, weights, band_gain):
    extent = tiles.shape[4]
    height = tiles.shape[3]
    holding = tiles.shape[2]
    peers = lax.axis_size("patch")
    depth = max(2, 2 * holding // peers)
    slots = peers * depth
    first_row = lax.axis_index("row") * height
    images = tiles[0, 0]
    target = targets[0, 0, :, 0]
    params = jnp.concatenate(
        [
            offsets[0, 0].astype(jnp.bfloat16),
            fractions[0, 0],
            kernels[0, 0].reshape(holding, 14),
            weights[0, 0][:, None],
        ],
        axis=1,
    )
    owner_hot = (target[:, None] == jnp.arange(peers)[None, :]).astype(jnp.int32)
    earlier = jnp.cumsum(owner_hot, axis=0) - owner_hot
    position = target * depth + jnp.sum(earlier * owner_hot, axis=1)
    placing = (position[None, :] == jnp.arange(slots)[:, None]).astype(jnp.bfloat16)

    def pack(values):
        flat = jnp.dot(placing, values.reshape(holding, -1), preferred_element_type=jnp.float32)
        return flat.astype(jnp.bfloat16).reshape((peers, depth) + values.shape[1:])

    slot_cols = None
    arrived, arrived_params = (
        lax.all_to_all(pack(images), "patch", split_axis=0, concat_axis=0, tiled=True),
        lax.all_to_all(pack(params), "patch", split_axis=0, concat_axis=0, tiled=True),
    )
    arrived_params = arrived_params.reshape(slots, 19)
    slot_cols = column_operator(arrived_params, extent)
    warped = warp_rows(
        arrived.reshape(slots, height, extent), arrived_params, slot_cols, first_row, extent
    )
    numer = source_sums(warped, arrived_params[:, 18], peers, depth).reshape(height, extent)
    slot_weight = arrived_params[:, 18]
    denom = 1.0 + jnp.sum(slot_weight.astype(jnp.float32))
    coadd = numer / denom
    coadd_low = coadd.astype(jnp.bfloat16)
    widened = with_halo(coadd_low, (("row", 0),), HALO)
    slot_templates = back_project(widened, arrived_params, slot_cols, first_row, extent)
    returned = lax.all_to_all(
        slot_templates.reshape(peers, depth, height, extent),
        "patch",
        split_axis=0,
        concat_axis=0,
        tiled=True,
    )
    templates = jnp.take(returned.reshape(slots, height, extent), position, axis=0)
    difference = (images.astype(jnp.float32) - templates.astype(jnp.float32)).astype(jnp.bfloat16)
    gained = band_gain[lax.axis_index("band")] * coadd
    share = height // lax.axis_size("band")
    total = lax.psum(gained.astype(jnp.bfloat16), "band").astype(jnp.float32)
    detection = lax.dynamic_slice_in_dim(total, lax.axis_index("band") * share, share, 0)
    return (coadd[None, None], detection[None], difference[None, None])


def solution(mesh):
    placed = (
        P(("tract", "band"), "patch", None, "row", None),
        P(("tract", "band"), "patch", None, None),
        P(("tract", "band"), "patch", None, None),
        P(("tract", "band"), "patch", None, None),
        P(("tract", "band"), "patch", None, None, None),
        P(("tract", "band"), "patch", None),
        P(),
    )
    return jax.shard_map(
        body,
        mesh=mesh,
        in_specs=placed,
        out_specs=(
            P(("tract", "band"), "patch", "row", None),
            P(("tract", "patch"), ("row", "band"), None),
            P(("tract", "band"), "patch", None, "row", None),
        ),
        check_vma=False,
    )
```

profile of v0, /device:TPU:0, one launch (start us, length us, event | category | flops | bytes accessed | tf_op | source)
XLA Modules:
  0.0 336.5 jit_solution(10615503652220454808)
XLA Ops:
  13.0 6.3 %all-to-all-start = ((bf16[4,2,152]{2,1,0:T(2,128)(2,1)}), bf16[4,2,152]{2,1,0:T(2,128)(2,1)S(1)}, u32[]{:S(2)}, u32[]{:S(2)}) async-start(bf16[4,2,152]{2,1,0:T(2,128)(2,1)} %reshape.2401), calls=%async_computation | async-start | bytes 8192 | tf_op jit(solution)/shard_map/all_to_all | solution.py:130
  30.0 2.8 copy.24
  34.0 3.0 copy.25
  37.0 5.1 %all-to-all-start.1 = ((bf16[4,16,128,256]{3,2,1,0:T(8,128)(2,1)}), bf16[4,16,128,256]{3,2,1,0:T(8,128)(2,1)}, u32[]{:S(2)}, u32[]{:S(2)}) async-start(bf16[4,16,128,256]{3,2,1,0:T(8,128)(2,1)} %bitcast.225), calls=%async_computation.1 | async-start | bytes 8388608 | tf_op jit(solution)/shard_map/all_to_all | solution.py:129
  42.9 1.4 multiply_add_fusion.1
  50.7 2.3 multiply_add_fusion
  53.1 57.6 %add_convert_fusion = bf16[64,256,256]{2,1,0:T(8,128)(2,1)} fusion(f32[64,256]{1,0:T(8,128)S(1)} %get-tuple-element.34, f32[64,256]{1,0:T(8,128)S(1)} %get-tuple-element.35, f32[64,256]{1,0:T(8,128)S(1)} %get-tuple-element.36, f32[64,256]{1,0:T(8,128)S(1)} %get-tuple-element.37, f32[64,256]{1,0:T(8,128)S(1)} %get-tuple-element.38, ...), kind=kLoop, calls=%fused_computation.2 | loop fusion | flops 192937984 | bytes 11403264 | tf_op jit(solution)/shard_map/convert_element_type | solution.py:58
  110.7 24.6 %all-to-all-done.1 = bf16[4,16,128,256]{3,2,1,0:T(8,128)(2,1)} async-done(((bf16[4,16,128,256]{3,2,1,0:T(8,128)(2,1)}), bf16[4,16,128,256]{3,2,1,0:T(8,128)(2,1)}, u32[]{:S(2)}, u32[]{:S(2)}) %all-to-all-start.1) | async-done | bytes 4194336 | tf_op jit(solution)/shard_map/all_to_all | solution.py:129
  135.7 7.5 %convolution_convert_fusion.1 = bf16[64,128,256]{2,1,0:T(8,128)(2,1)S(1)} fusion(bf16[64,128,256]{2,1,0:T(8,128)(2,1)} %bitcast.37, bf16[64,256,256]{2,1,0:T(8,128)(2,1)} %add_convert_fusion), kind=kOutput, calls=%fused_computation.17 | convolution fusion | flops 1075838976 | bytes 16777216 | tf_op jit(solution)/shard_map/nrj,nij->nri/dot_general | solution.py:64
  144.7 1.5 collective-permute-start.1
  146.4 2.1 collective-permute-done.1
  148.9 17.0 %fusion.13 = bf16[64,128,256]{2,1,0:T(8,128)(2,1)} fusion(bf16[64,12,256]{2,1,0:T(8,128)(2,1)S(1)} %collective-permute-done.1, bf16[64,128,256]{2,1,0:T(8,128)(2,1)S(1)} %convolution_convert_fusion.1, bf16[64,12,256]{2,1,0:T(8,128)(2,1)S(1)} %collective-permute-done, f32[64,128]{1,0:T(8,128)S(1)} %copy-done.5, f32[64,128]{1,0:T(8,128)S(1)} %copy-done.6, ...), kind=kOutput, calls=%fused_computation.16 | convolution fusion | flops 711852032 | bytes 10376192 | tf_op jit(solution)/shard_map/nim,nmc->nic/dot_general | solution.py:72
  166.0 7.4 %reshape.2378 = bf16[4,16,32768]{2,1,0:T(8,128)(2,1)} reshape(bf16[64,128,256]{2,1,0:T(8,128)(2,1)} %fusion.13) | data formatting | bytes 8388608 | tf_op jit(solution)/shard_map/reshape | solution.py:92
  173.5 3.0 fusion.303
  177.2 2.6 collective-permute-start.2
  179.8 1.5 collective-permute-start.3
  181.5 1.6 collective-permute-done.3
  183.2 32.8 %fusion.313 = bf16[64,128,256]{2,1,0:T(8,128)(2,1)S(1)} fusion(f32[64,152]{1,0:T(8,128)S(1)} %get-tuple-element.11, f32[64,152]{1,0:T(8,128)S(1)} %get-tuple-element.12, f32[64,152]{1,0:T(8,128)S(1)} %get-tuple-element.13, f32[64,152]{1,0:T(8,128)S(1)} %get-tuple-element.14, f32[64,152]{1,0:T(8,128)S(1)} %get-tuple-element.15, ...), kind=kOutput, calls=%fused_computation.13.clone.clone.clone.1 | convolution fusion | flops 697143296 | bytes 5614592 | tf_op jit(solution)/shard_map/nij,ic->njc/dot_general | solution.py:84
  216.0 6.7 %fusion.10 = bf16[64,128,256]{2,1,0:T(8,128)(2,1)} fusion(bf16[64,256,256]{2,1,0:T(8,128)(2,1)} %add_convert_fusion, bf16[64,128,256]{2,1,0:T(8,128)(2,1)S(1)} %fusion.313), kind=kOutput, calls=%fused_computation.15 | convolution fusion | flops 1075838976 | bytes 16777216 | tf_op jit(solution)/shard_map/nji,nic->njc/dot_general | solution.py:86
  222.7 5.0 %all-to-all-start.2 = ((bf16[4,16,128,256]{3,2,1,0:T(8,128)(2,1)}), bf16[4,16,128,256]{3,2,1,0:T(8,128)(2,1)}, u32[]{:S(2)}, u32[]{:S(2)}) async-start(bf16[4,16,128,256]{3,2,1,0:T(8,128)(2,1)} %bitcast.224), calls=%async_computation.2 | async-start | bytes 8388608 | tf_op jit(solution)/shard_map/all_to_all | solution.py:144
  230.4 23.2 %all-reduce.2.cloned.1.call-done = bf16[128,256]{1,0:T(8,128)(2,1)} async-done(((bf16[128,256]{1,0:T(8,128)(2,1)}), bf16[128,256]{1,0:T(8,128)(2,1)}) %all-reduce.2.cloned.1.call-update) | async-done | bytes 65552 | tf_op jit(solution)/shard_map/psum | solution.py:155
  255.0 66.5 %all-to-all-done.2 = bf16[4,16,128,256]{3,2,1,0:T(8,128)(2,1)} async-done(((bf16[4,16,128,256]{3,2,1,0:T(8,128)(2,1)}), bf16[4,16,128,256]{3,2,1,0:T(8,128)(2,1)}, u32[]{:S(2)}, u32[]{:S(2)}) %all-to-all-start.2) | async-done | bytes 4194336 | tf_op jit(solution)/shard_map/all_to_all | solution.py:144
  321.5 4.2 %gather_fusion = bf16[32,128,256]{2,1,0:T(8,128)(2,1)} fusion(bf16[64,128,256]{2,1,0:T(8,128)(2,1)} %bitcast.97, s32[1024]{0:T(1024)S(1)} %pad_clamp_fusion), kind=kCustom, calls=%fused_computation | custom fusion | bytes 4194432 | tf_op jit(solution)/shard_map/jit(_take)/gather | solution.py:151
  325.7 3.9 %subtract_convert_fusion = bf16[1,1,32,128,256]{4,3,2,1,0:T(8,128)(2,1)} fusion(bf16[1,1,32,128,256]{4,3,2,1,0:T(8,128)(2,1)S(1)} %copy-done, bf16[32,128,256]{2,1,0:T(8,128)(2,1)} %gather_fusion, pred[32]{0:T(512)(128)(4,1)S(1)} %copy-done.61), kind=kLoop, calls=%fused_computation.11 | loop fusion | flops 5242880 | bytes 6291488 | tf_op jit(solution)/shard_map/convert_element_type | solution.py:152
  (227 shorter events, 30.6 us)
Async XLA Ops:
  13.0 24.0 %all-to-all-start = ((bf16[4,2,152]{2,1,0:T(2,128)(2,1)}), bf16[4,2,152]{2,1,0:T(2,128)(2,1)S(1)}, u32[]{:S(2)}, u32[]{:S(2)}) async-start(bf16[4,2,152]{2,1,0:T(2,128)(2,1)} %reshape.2401), calls=%async_computation | async-start | bytes 8192 | tf_op jit(solution)/shard_map/all_to_all | solution.py:130
  37.0 98.3 %all-to-all-start.1 = ((bf16[4,16,128,256]{3,2,1,0:T(8,128)(2,1)}), bf16[4,16,128,256]{3,2,1,0:T(8,128)(2,1)}, u32[]{:S(2)}, u32[]{:S(2)}) async-start(bf16[4,16,128,256]{3,2,1,0:T(8,128)(2,1)} %bitcast.225), calls=%async_computation.1 | async-start | bytes 8388608 | tf_op jit(solution)/shard_map/all_to_all | solution.py:129
  135.3 13.3 %copy-start.8 = (f32[64,128]{1,0:T(8,128)S(1)}, f32[64,128]{1,0:T(8,128)}, u32[]{:S(2)}) copy-start(f32[64,128]{1,0:T(8,128)} %get-tuple-element.60) | copy-start | bytes 98308
  135.3 13.3 %copy-start.9 = (f32[64,128]{1,0:T(8,128)S(1)}, f32[64,128]{1,0:T(8,128)}, u32[]{:S(2)}) copy-start(f32[64,128]{1,0:T(8,128)} %get-tuple-element.61) | copy-start | bytes 98308
  135.3 13.3 %copy-start.10 = (f32[64,128]{1,0:T(8,128)S(1)}, f32[64,128]{1,0:T(8,128)}, u32[]{:S(2)}) copy-start(f32[64,128]{1,0:T(8,128)} %get-tuple-element.62) | copy-start | bytes 98308
  135.3 13.3 %copy-start.11 = (f32[64,128]{1,0:T(8,128)S(1)}, f32[64,128]{1,0:T(8,128)}, u32[]{:S(2)}) copy-start(f32[64,128]{1,0:T(8,128)} %get-tuple-element.63) | copy-start | bytes 98308
  135.4 13.3 %copy-start.12 = (f32[64,128]{1,0:T(8,128)S(1)}, f32[64,128]{1,0:T(8,128)}, u32[]{:S(2)}) copy-start(f32[64,128]{1,0:T(8,128)} %get-tuple-element.64) | copy-start | bytes 98308
  135.4 13.3 %copy-start.13 = (f32[64,128]{1,0:T(8,128)S(1)}, f32[64,128]{1,0:T(8,128)}, u32[]{:S(2)}) copy-start(f32[64,128]{1,0:T(8,128)} %get-tuple-element.65) | copy-start | bytes 98308
  135.4 13.3 %copy-start.14 = (f32[64,128]{1,0:T(8,128)S(1)}, f32[64,128]{1,0:T(8,128)}, u32[]{:S(2)}) copy-start(f32[64,128]{1,0:T(8,128)} %get-tuple-element.66) | copy-start | bytes 98308
  135.4 13.3 %copy-start.15 = (f32[64,128]{1,0:T(8,128)S(1)}, f32[64,128]{1,0:T(8,128)}, u32[]{:S(2)}) copy-start(f32[64,128]{1,0:T(8,128)} %get-tuple-element.67) | copy-start | bytes 98308
  135.4 13.3 %copy-start.16 = (f32[64,128]{1,0:T(8,128)S(1)}, f32[64,128]{1,0:T(8,128)}, u32[]{:S(2)}) copy-start(f32[64,128]{1,0:T(8,128)} %get-tuple-element.68) | copy-start | bytes 98308
  135.4 13.3 %copy-start.17 = (f32[64,128]{1,0:T(8,128)S(1)}, f32[64,128]{1,0:T(8,128)}, u32[]{:S(2)}) copy-start(f32[64,128]{1,0:T(8,128)} %get-tuple-element.69) | copy-start | bytes 98308
  135.4 13.3 %copy-start.18 = (f32[64,128]{1,0:T(8,128)S(1)}, f32[64,128]{1,0:T(8,128)}, u32[]{:S(2)}) copy-start(f32[64,128]{1,0:T(8,128)} %get-tuple-element.70) | copy-start | bytes 98308
  135.4 13.3 %copy-start.19 = (f32[64,128]{1,0:T(8,128)S(1)}, f32[64,128]{1,0:T(8,128)}, u32[]{:S(2)}) copy-start(f32[64,128]{1,0:T(8,128)} %get-tuple-element.71) | copy-start | bytes 98308
  135.4 13.3 %copy-start.20 = (f32[64,128]{1,0:T(8,128)S(1)}, f32[64,128]{1,0:T(8,128)}, u32[]{:S(2)}) copy-start(f32[64,128]{1,0:T(8,128)} %get-tuple-element.72) | copy-start | bytes 98308
  135.4 13.3 %copy-start.21 = (f32[64,128]{1,0:T(8,128)S(1)}, f32[64,128]{1,0:T(8,128)}, u32[]{:S(2)}) copy-start(f32[64,128]{1,0:T(8,128)} %get-tuple-element.73) | copy-start | bytes 98308
  143.4 3.0 collective-permute-start
  144.7 3.8 %collective-permute-start.1 = (bf16[64,12,256]{2,1,0:T(8,128)(2,1)S(1)}, bf16[64,12,256]{2,1,0:T(8,128)(2,1)S(1)}, u32[]{:S(2)}, u32[]{:S(2)}) collective-permute-start(bf16[64,12,256]{2,1,0:T(8,128)(2,1)S(1)} %get-tuple-element.9), channel_id=1, source_target_pairs={{1,0},{3,2},{5,4},{7,6},{9,8},{11,10},{13,12},{15,14},{17,16},{19,... | collective-permute-start | bytes 1179656 | tf_op jit(solution)/shard_map/ppermute | solution.py:20
  177.2 4.2 %collective-permute-start.2 = (bf16[12,256]{1,0:T(8,128)(2,1)S(1)}, bf16[12,256]{1,0:T(8,128)(2,1)}, u32[]{:S(2)}, u32[]{:S(2)}) collective-permute-start(bf16[12,256]{1,0:T(8,128)(2,1)S(1)} %slice.505), channel_id=1, source_target_pairs={{0,1},{2,3},{4,5},{6,7},{8,9},{10,11},{12,13},{14,15},{16,17},{18,... | collective-permute-start | bytes 18440 | tf_op jit(solution)/shard_map/ppermute | solution.py:17
  179.8 3.2 collective-permute-start.3
  222.7 103.0 %copy-start = (bf16[1,1,32,128,256]{4,3,2,1,0:T(8,128)(2,1)S(1)}, bf16[1,1,32,128,256]{4,3,2,1,0:T(8,128)(2,1)}, u32[]{:S(2)}) copy-start(bf16[1,1,32,128,256]{4,3,2,1,0:T(8,128)(2,1)} %param.8) | copy-start | bytes 6291460
  222.7 103.0 %copy-start.61 = (pred[32]{0:T(512)(128)(4,1)S(1)}, pred[32]{0:T(512)(128)(4,1)}, u32[]{:S(2)}) copy-start(pred[32]{0:T(512)(128)(4,1)} %get-tuple-element.4) | copy-start | bytes 100
  222.7 98.8 %all-to-all-start.2 = ((bf16[4,16,128,256]{3,2,1,0:T(8,128)(2,1)}), bf16[4,16,128,256]{3,2,1,0:T(8,128)(2,1)}, u32[]{:S(2)}, u32[]{:S(2)}) async-start(bf16[4,16,128,256]{3,2,1,0:T(8,128)(2,1)} %bitcast.224), calls=%async_computation.2 | async-start | bytes 8388608 | tf_op jit(solution)/shard_map/all_to_all | solution.py:144
  227.7 25.9 %all-reduce.2.cloned.1.call-start = ((), (), s32[]{:S(2)}) async-start(), calls=%async_computation.3 | async-start | bytes 131072 | tf_op jit(solution)/shard_map/psum | solution.py:155
  (49 other events, 533.9 us)
Sparse Core Ops, SparseCore 0:
  231.4 22.1 all-reduce.1
where the time goes:
time: 338 us; the launch traced here: 336 us
  waiting for transfers between devices  118 us (35%)
  other arithmetic  85.8 us (25%)
  matrix products  69.2 us (20%)
  local copies, waits for them, and re-layouts  24 us (7%)
  starting transfers between devices  23.4 us (7%)
  between operations  16 us (5%)
    all_to_all x1, waiting for transfers between devices, body(): lax.all_to_all(slot_templates.reshape(peers, depth, height, extent), 'pat...  66.5 us
    convert_element_type x1, other arithmetic, column_operator(): return spread(band, rows, rows).astype(jnp.bfloat16)  57.6 us
    dot_general x1, matrix products, back_project(): jnp.einsum('nij,ic->njc', row_op, extended, preferred_element_type=jnp.fl...  32.8 us
    all_to_all x1, waiting for transfers between devices, body(): lax.all_to_all(pack(images), 'patch', split_axis=0, concat_axis=0, tiled=...  24.6 us
    psum x1, waiting for transfers between devices, body(): total = lax.psum(gained.astype(jnp.bfloat16), 'band').astype(jnp.float32)  23.2 us
    dot_general x1, matrix products, warp_rows(): jnp.einsum('nim,nmc->nic', row_op, extended, preferred_element_type=jnp.f...  17 us
    eq x14, other arithmetic, spread(): lagged == number - reach  10.3 us
    unnamed x135, local copies, waits for them, and re-layouts  7.55 us
  transfers between devices with their start and end apart: 8, of which 5 were waited for; matrix products, arithmetic and copies ran while one was open for 27% of the time, Pallas kernels for 0%

commit v1 on v0

v1 whole, which is shorter than its diff:
```python
import functools
import math

import jax
import jax.numpy as jnp
from jax import lax
from jax.experimental import pallas as pl
from jax.experimental.pallas import tpu as pltpu
from jax.sharding import PartitionSpec as P

EDGE = 16
MESH = pl.DeviceIdType.MESH


def lanczos(x):
    w = (x * x) * jnp.float32((math.pi / 3.0) ** 2)
    q = jnp.full_like(w, (-1.0) ** 10 / math.factorial(21))
    for k in range(9, -1, -1):
        q = q * w + jnp.float32((-1.0) ** k / math.factorial(2 * k + 1))
    q2 = q * q
    value = q2 * (1.0 - jnp.float32(4.0 / 3.0) * w * q2)
    return jnp.where(jnp.abs(x) < 3.0, value, 0.0)


def skewed(shift, taps):
    row = lax.broadcasted_iota(jnp.int32, (8, 128), 0)
    lane = lax.broadcasted_iota(jnp.int32, (8, 128), 1)
    lag = (lane - 64 - row).astype(jnp.float32)
    table = lanczos(lag - shift)
    mid = top = bottom = None
    for d in range(-3, 4):
        term = taps(d + 3) * (table if d == 0 else pltpu.roll(table, d % 128, 1))
        term_top = term if d >= 0 else jnp.where(row + d >= 0, term, 0.0)
        term_bottom = term if d <= 0 else jnp.where(row + d < 8, term, 0.0)
        mid = term if mid is None else mid + term
        top = term_top if top is None else top + term_top
        bottom = term_bottom if bottom is None else bottom + term_bottom
    return top, mid, bottom


def place(block, k):
    amount = (8 * k - 64) % 128
    return block if amount == 0 else pltpu.roll(block, amount, 1)


def low_half(block):
    lane = lax.broadcasted_iota(jnp.int32, block.shape, 1)
    return jnp.where(lane < 64, block, 0.0)


def high_half(block):
    lane = lax.broadcasted_iota(jnp.int32, block.shape, 1)
    return jnp.where(lane >= 64, block, 0.0)


def pair(first, second):
    return jnp.concatenate([first, second], axis=0).astype(jnp.bfloat16)


def build_columns(params_ref, t, put):
    top, mid, bottom = skewed(params_ref[t, 0], lambda d: params_ref[t, 2 + d])
    rolled = [place(mid, k) for k in range(16)]
    blocks = rolled + rolled
    blocks[0], blocks[31] = place(top, 0), place(bottom, 31)
    for q in range(16):
        both = blocks[2 * q], blocks[2 * q + 1]
        if q <= 8:
            f = low_half if q in (0, 8) else (high_half if q == 7 else (lambda b: b))
            left = [high_half(b) for b in both] if q in (7, 8) else [f(b) for b in both]
            put(q, 0, pair(*left))
        if q >= 7:
            if q in (7, 8):
                right = [low_half(b) for b in both]
            elif q == 15:
                right = [high_half(b) for b in both]
            else:
                right = both
            put(q, 1, pair(*right))


def build_rows(params_ref, t, side, scale, put):
    top, mid, bottom = skewed(params_ref[t, 1], lambda d: params_ref[t, 9 + d])
    if scale is not None:
        top, mid, bottom = top * scale, mid * scale, bottom * scale
    upper = side == 0
    first = jnp.where(upper, top, mid)
    last = jnp.where(upper, mid, bottom)
    blocks = [place(first, 0)] + [place(mid, k) for k in range(1, 15)] + [place(last, 15)]
    for q in range(8):
        both = blocks[2 * q], blocks[2 * q + 1]
        if q == 0:
            both = [low_half(b) for b in both]
        if q == 7:
            both = [high_half(b) for b in both]
        put(q, pair(*both))
    below = [high_half(place(mid, 16 + h)) for h in range(2)]
    above = [low_half(place(mid, h - 2)) for h in range(2)]
    put(8, pair(*[jnp.where(upper, b, a) for b, a in zip(below, above)]))


def forward_kernel(
    patches, group, params_ref, targets_ref, tiles_ref, main_ref, edge_ref,
    cols_ref, rows_ref, section_ref, mask_ref, den_ref,
):
    step = pl.program_id(0)
    side = lax.axis_index("row")
    height = tiles_ref.shape[1]

    @pl.when(step == 0)
    def _():
        cols_ref[...] = jnp.zeros_like(cols_ref)
        den_ref[...] = jnp.zeros_like(den_ref)

    index = lax.broadcasted_iota(jnp.int32, den_ref.shape, 0)
    for g in range(group):
        t = step * group + g
        weight = params_ref[t, 16]

        def put_col(q, half, tile):
            cols_ref[g, 16 * q : 16 * q + 16, 128 * half : 128 * half + 128] = tile

        def put_row(q, tile):
            rows_ref[16 * q : 16 * q + 16, pl.ds(pl.multiple_of(t * 128, 128), 128)] = tile

        build_columns(params_ref, t, put_col)
        build_rows(params_ref, t, side, weight, put_row)
        section = lax.dot_general(
            tiles_ref[g], cols_ref[g], (((1,), (1,)), ((), ())), preferred_element_type=jnp.float32
        )
        section_ref[pl.ds(pl.multiple_of(t * height, height), height), :] = section.astype(jnp.bfloat16)
        chosen = index == targets_ref[t, 0]
        mask_ref[:, pl.ds(pl.multiple_of(t * 128, 128), 128)] = jnp.where(chosen, 1.0, 0.0)
        den_ref[...] += jnp.where(chosen, weight, 0.0)

    @pl.when(step == pl.num_programs(0) - 1)
    def _():
        @pl.loop(0, patches)
        def _(p):
            mask = mask_ref[pl.ds(p, 1), :].astype(jnp.bfloat16)
            total = jnp.dot(
                rows_ref[...] * mask, section_ref[...], preferred_element_type=jnp.float32
            ).astype(jnp.bfloat16)
            main_ref[p, :height] = total[:height]
            edge_ref[p] = total[height:]
            den = den_ref[pl.ds(p, 1), :]
            den = jnp.concatenate([den, den], axis=1)
            high = den.astype(jnp.bfloat16).astype(jnp.float32)
            line = lax.broadcasted_iota(jnp.int32, (EDGE, 256), 0)
            parts = jnp.where(line == 0, high, jnp.where(line == 1, den - high, 0.0))
            main_ref[p, height:] = parts.astype(jnp.bfloat16)


def exchange_kernel(
    patches, bands, gain_ref, main_ref, edge_ref, coadd_ref, detection_ref, low_ref,
    main_in, edge_in, low_in, near_in, low_out, gained_out, gained_in,
    main_send, main_recv, edge_send, edge_recv, low_send, low_recv, near_send, near_recv,
    band_send, band_recv,
):
    me = lax.axis_index("patch")
    band = lax.axis_index("band")
    side = lax.axis_index("row")
    height, share = coadd_ref.shape[0], detection_ref.shape[0]
    across = 1 - side
    edge_at = pl.multiple_of((1 - side) * (height - EDGE), EDGE)

    barrier = pltpu.get_barrier_semaphore()
    others = [lax.rem(me + k, patches) for k in range(1, patches)]
    everyone = [me] + others
    partners = [lax.rem(band + k, bands) for k in range(1, bands)]
    for z in others:
        pl.semaphore_signal(barrier, inc=1, device_id={"patch": z}, device_id_type=MESH)
    for z in everyone:
        pl.semaphore_signal(
            barrier, inc=1, device_id={"patch": z, "row": across}, device_id_type=MESH
        )
    for b in partners:
        pl.semaphore_signal(barrier, inc=1, device_id={"band": b}, device_id_type=MESH)
    pl.semaphore_wait(barrier, 2 * patches - 1 + bands - 1)

    def remote(source, place_at, send, recv, where):
        return pltpu.make_async_remote_copy(
            src_ref=source, dst_ref=place_at, send_sem=send, recv_sem=recv,
            device_id=where, device_id_type=MESH,
        )

    copies = []
    for k in range(1, patches):
        z = lax.rem(me + k, patches)
        copies.append(remote(main_ref.at[z], main_in.at[k], main_send.at[k], main_recv.at[k], {"patch": z}))
    for k in range(patches):
        z = lax.rem(me + k, patches)
        copies.append(
            remote(edge_ref.at[z], edge_in.at[k], edge_send.at[k], edge_recv.at[k], {"patch": z, "row": across})
        )
    for copy in copies:
        copy.start()
    for copy in copies:
        copy.wait()

    total = main_ref[me].astype(jnp.float32)
    near = edge_in[0].astype(jnp.float32)
    for k in range(1, patches):
        total += main_in[k].astype(jnp.float32)
        near += edge_in[k].astype(jnp.float32)
    den = 1.0 + jnp.sum(total[height:], axis=0, keepdims=True)
    coadd_ref[...] = total[:height] / den
    coadd_ref[pl.ds(edge_at, EDGE), :] += near / den
    coadd = coadd_ref[...]
    low_out[...] = coadd.astype(jnp.bfloat16)
    gained = gain_ref[band] * coadd
    gained_out[...] = gained.astype(jnp.bfloat16)

    copies = []
    for k in range(1, patches):
        z = lax.rem(me + k, patches)
        copies.append(remote(low_out, low_in.at[k], low_send.at[k], low_recv.at[k], {"patch": z}))
    for k in range(patches):
        z = lax.rem(me + k, patches)
        copies.append(
            remote(
                low_out.at[pl.ds(edge_at, EDGE)], near_in.at[k], near_send.at[k], near_recv.at[k],
                {"patch": z, "row": across},
            )
        )
    for k in range(1, bands):
        b = lax.rem(band + k, bands)
        copies.append(
            remote(
                gained_out.at[pl.ds(pl.multiple_of(b * share, EDGE), share)], gained_in.at[k],
                band_send.at[k], band_recv.at[k], {"band": b},
            )
        )
    for copy in copies:
        copy.start()
    low_ref[me, :height] = low_out[...]
    for copy in copies:
        copy.wait()
    detection = gain_ref[band] * coadd_ref[pl.ds(pl.multiple_of(band * share, EDGE), share), :]
    for k in range(1, bands):
        detection += gained_in[k].astype(jnp.float32)
    detection_ref[...] = detection
    for k in range(patches):
        z = lax.rem(me - k + patches, patches)
        if k > 0:
            low_ref[z, :height] = low_in[k]
        low_ref[z, height:] = near_in[k]


def backward_kernel(group, params_ref, targets_ref, tiles_ref, low_ref, out_ref, cols_ref, rows_ref):
    step = pl.program_id(0)
    side = lax.axis_index("row")

    @pl.when(step == 0)
    def _():
        cols_ref[...] = jnp.zeros_like(cols_ref)

    for g in range(group):
        t = step * group + g

        def put_col(q, half, tile):
            cols_ref[g, 16 * q : 16 * q + 16, 128 * half : 128 * half + 128] = tile

        def put_row(q, tile):
            rows_ref[g, 16 * q : 16 * q + 16, :] = tile

        build_columns(params_ref, t, put_col)
        build_rows(params_ref, t, side, None, put_row)
        back = lax.dot_general(
            rows_ref[g], low_ref[targets_ref[t, 0]], (((0,), (0,)), ((), ())),
            preferred_element_type=jnp.float32,
        ).astype(jnp.bfloat16)
        template = jnp.dot(back, cols_ref[g], preferred_element_type=jnp.float32)
        template = template.astype(jnp.bfloat16).astype(jnp.float32)
        out_ref[g] = (tiles_ref[g].astype(jnp.float32) - template).astype(jnp.bfloat16)


def body(tiles, targets, offsets, fractions, kernels, weights, band_gain):
    holding, height, extent = tiles.shape[2:]
    patches, bands = lax.axis_size("patch"), lax.axis_size("band")
    images, target = tiles[0, 0], targets[0, 0]
    params = jnp.concatenate(
        [
            offsets[0, 0].astype(jnp.float32) + fractions[0, 0].astype(jnp.float32),
            kernels[0, 0].reshape(holding, 14).astype(jnp.float32),
            weights[0, 0][:, None].astype(jnp.float32),
        ],
        axis=1,
    )
    smem = pl.BlockSpec(memory_space=pltpu.SMEM)
    vmem = pl.BlockSpec(memory_space=pltpu.VMEM)
    group = 8
    padded = -(-patches // 8) * 8
    tile_spec = pl.BlockSpec((group, height, extent), lambda i: (i, 0, 0))
    whole = lambda *shape: pl.BlockSpec(shape, lambda i: (0,) * len(shape))
    macs = holding * height * extent * extent
    main, edge = pl.pallas_call(
        functools.partial(forward_kernel, patches, group),
        grid=(holding // group,),
        in_specs=[smem, smem, tile_spec],
        out_specs=[whole(patches, height + EDGE, extent), whole(patches, EDGE, extent)],
        out_shape=[
            jax.ShapeDtypeStruct((patches, height + EDGE, extent), jnp.bfloat16),
            jax.ShapeDtypeStruct((patches, EDGE, extent), jnp.bfloat16),
        ],
        scratch_shapes=[
            pltpu.VMEM((group, extent, extent), jnp.bfloat16),
            pltpu.VMEM((height + EDGE, holding * 128), jnp.bfloat16),
            pltpu.VMEM((holding * height, extent), jnp.bfloat16),
            pltpu.VMEM((padded, holding * 128), jnp.float32),
            pltpu.VMEM((padded, 128), jnp.float32),
        ],
        compiler_params=pltpu.CompilerParams(vmem_limit_bytes=40 << 20),
        cost_estimate=pl.CostEstimate(flops=2 * macs * 4, bytes_accessed=3 << 20, transcendentals=0),
        name="forward",
    )(params, target, images)

    share = height // bands
    dma = pltpu.SemaphoreType.DMA
    coadd, detection, low = pl.pallas_call(
        functools.partial(exchange_kernel, patches, bands),
        in_specs=[smem, vmem, vmem],
        out_specs=[vmem, vmem, vmem],
        out_shape=[
            jax.ShapeDtypeStruct((height, extent), jnp.float32),
            jax.ShapeDtypeStruct((share, extent), jnp.float32),
            jax.ShapeDtypeStruct((patches, height + EDGE, extent), jnp.bfloat16),
        ],
        scratch_shapes=[
            pltpu.VMEM((patches, height + EDGE, extent), jnp.bfloat16),
            pltpu.VMEM((patches, EDGE, extent), jnp.bfloat16),
            pltpu.VMEM((patches, height, extent), jnp.bfloat16),
            pltpu.VMEM((patches, EDGE, extent), jnp.bfloat16),
            pltpu.VMEM((height, extent), jnp.bfloat16),
            pltpu.VMEM((height, extent), jnp.bfloat16),
            pltpu.VMEM((bands, share, extent), jnp.bfloat16),
        ]
        + [dma((patches,))] * 8
        + [dma((bands,))] * 2,
        compiler_params=pltpu.CompilerParams(
            collective_id=0, has_side_effects=True, vmem_limit_bytes=40 << 20
        ),
        cost_estimate=pl.CostEstimate(flops=1 << 20, bytes_accessed=2 << 20, transcendentals=0),
        name="exchange",
    )(band_gain, main, edge)

    difference = pl.pallas_call(
        functools.partial(backward_kernel, group),
        grid=(holding // group,),
        in_specs=[smem, smem, tile_spec, whole(patches, height + EDGE, extent)],
        out_specs=tile_spec,
        out_shape=jax.ShapeDtypeStruct((holding, height, extent), jnp.bfloat16),
        scratch_shapes=[
            pltpu.VMEM((group, extent, extent), jnp.bfloat16),
            pltpu.VMEM((group, height + EDGE, 128), jnp.bfloat16),
        ],
        compiler_params=pltpu.CompilerParams(vmem_limit_bytes=40 << 20),
        cost_estimate=pl.CostEstimate(flops=4 * macs, bytes_accessed=5 << 20, transcendentals=0),
        name="backward",
    )(params, target, images, low)
    return (coadd[None, None], detection[None], difference[None, None])


def solution(mesh):
    placed = (
        P(("tract", "band"), "patch", None, "row", None),
        P(("tract", "band"), "patch", None, None),
        P(("tract", "band"), "patch", None, None),
        P(("tract", "band"), "patch", None, None),
        P(("tract", "band"), "patch", None, None, None),
        P(("tract", "band"), "patch", None),
        P(),
    )
    return jax.shard_map(
        body,
        mesh=mesh,
        in_specs=placed,
        out_specs=(
            P(("tract", "band"), "patch", "row", None),
            P(("tract", "patch"), ("row", "band"), None),
            P(("tract", "band"), "patch", None, "row", None),
        ),
        check_vma=False,
    )
```

time: 338 us -> 43.9 us (0.13)
  waiting for transfers between devices: 118 us -> 0 us
  other arithmetic: 85.8 us -> 1.43 us
  matrix products: 69.2 us -> 0 us
  Pallas kernels: 0 us -> 37 us
  starting transfers between devices: 23.4 us -> 0 us
  local copies, waits for them, and re-layouts: 24 us -> 4.57 us
  between operations: 16 us -> 0.67 us
    all_to_all x3 -> x0, waiting for transfers between devices: 91.2 us -> none  [the longest x1 66.5 us: body(): lax.all_to_all(slot_templates.reshape(peers, depth, height, extent), 'pat...]
    dot_general x7 -> x0, matrix products: 69.2 us -> none  [the longest x1 32.8 us: back_project(): jnp.einsum('nij,ic->njc', row_op, extended, preferred_element_type=jnp.fl...]
    convert_element_type x29 -> x1, other arithmetic: 63.7 us -> 0.66 us  [body(): weights[0, 0][:, None].astype(jnp.float32)]
    pallas_call x0 -> x3, Pallas kernels: none -> 37 us  [the longest x1 22.6 us: body(): pl.pallas_call(functools.partial(exchange_kernel, patches, bands), in_spe...]
    psum x1 -> x0, waiting for transfers between devices: 23.2 us -> none  [body(): total = lax.psum(gained.astype(jnp.bfloat16), 'band').astype(jnp.float32)]
    all_to_all x3 -> x0, starting transfers between devices: 16.4 us -> none  [the longest x1 6.32 us: body(): lax.all_to_all(pack(params), 'patch', split_axis=0, concat_axis=0, tiled=...]
    eq x14 -> x0, other arithmetic: 10.3 us -> none  [spread(): lagged == number - reach]
    reshape x3 -> x0, local copies, waits for them, and re-layouts: 7.61 us -> none  [the longest x1 7.41 us: source_sums(): flat = warped.reshape(peers, depth, -1)]
  transfers between devices with their start and end apart: 8 -> 0, of which waited for: 5 -> 0; matrix products, arithmetic and copies ran while one was open for 27% -> 0% of each run, Pallas kernels for 0% -> 0%
where the time goes in v1:
time: 43.9 us; the launch traced here: 43.7 us
  Pallas kernels  37 us (84%)
  local copies, waits for them, and re-layouts  4.57 us (10%)
  other arithmetic  1.43 us (3%)
  between operations  0.67 us (2%)
    pallas_call x1, Pallas kernels, body(): pl.pallas_call(functools.partial(exchange_kernel, patches, bands), in_spe...  22.6 us
    pallas_call x1, Pallas kernels, body(): pl.pallas_call(functools.partial(forward_kernel, patches, group), grid=(h...  7.69 us
    pallas_call x1, Pallas kernels, body(): pl.pallas_call(functools.partial(backward_kernel, group), grid=(holding /...  6.74 us
    unnamed x8, local copies, waits for them, and re-layouts  2.88 us

profile of v1, /device:TPU:0, one launch (start us, length us, event | category | flops | bytes accessed | tf_op | source)
XLA Modules:
  0.0 43.7 jit_solution(160177518930799138)
XLA Ops:
  0.6 0.7 %bitcast_convert_fusion = f32[32,1]{0,1:T(1,128)S(1)} fusion(bf16[1,1,32]{2,1,0:T(2,128)(2,1)} %param.12), kind=kLoop, calls=%fused_computation.2 | loop fusion | flops 32 | bytes 192 | tf_op jit(solution)/shard_map/convert_element_type | solution.py:285
  1.3 0.7 %add_bitcast_fusion = f32[32,2]{0,1:T(2,128)S(1)} fusion(bf16[1,1,32,2]{2,3,1,0:T(2,128)(2,1)} %param.10, s32[1,1,32,2]{2,3,1,0:T(2,128)} %param.9), kind=kLoop, calls=%fused_computation.1 | loop fusion | flops 192 | bytes 640 | tf_op jit(solution)/shard_map/add | solution.py:283
  2.0 0.7 %copy.15 = f32[1,1,32,2,7]{2,4,3,1,0:T(8,128)S(1)} copy(bf16[1,1,32,2,7]{2,3,4,1,0:T(2,128)(2,1)} %param.11) | data formatting | bytes 2688 | tf_op jit(solution)/shard_map/convert_element_type | solution.py:284
  2.7 0.1 copy.17
  2.8 0.1 copy.16
  2.9 0.1 copy.18
  2.9 0.1 pad_maximum_fusion.params_ref
  3.0 0.7 %copy.19.targets_ref = s32[32,1]{1,0:T(8,128)S(1)} copy(s32[32,1]{0,1:T(1,128)} %bitcast.17) | data formatting | bytes 256 | tf_op jit(solution)/shard_map/squeeze | solution.py:280
  3.8 0.0 copy-start
  3.8 1.6 %copy-done = bf16[1,1,32,128,256]{4,3,2,1,0:T(8,128)(2,1)S(1)} copy-done((bf16[1,1,32,128,256]{4,3,2,1,0:T(8,128)(2,1)S(1)}, bf16[1,1,32,128,256]{4,3,2,1,0:T(8,128)(2,1)}, u32[]{:S(2)}) %copy-start) | copy-done | bytes 2097176
  5.4 0.0 copy-start.2
  5.4 0.0 copy-start.1
  5.4 7.7 %forward.1 = (bf16[4,144,256]{2,1,0:T(8,128)(2,1)S(1)}, bf16[4,16,256]{2,1,0:T(8,128)(2,1)S(1)}) custom-call(f32[32,17]{1,0:T(8,128)S(1)} %pad_maximum_fusion.params_ref, s32[32,1]{1,0:T(8,128)S(1)} %copy.19.targets_ref, bf16[32,128,256]{2,1,0:T(8,128)(2,1)S(1)} %bitcast.12), custom_call_target="tpu_custom_call" | custom-call | flops 2147483648 | bytes 3145728 | tf_op jit(solution)/shard_map/forward/pallas_call | solution.py:296
  13.1 0.0 copy-done.2
  13.1 22.6 %exchange.1 = (f32[128,256]{1,0:T(8,128)S(1)}, f32[64,256]{1,0:T(8,128)S(1)}, bf16[4,144,256]{2,1,0:T(8,128)(2,1)S(1)}) custom-call(f32[2]{0:T(128)S(1)} %copy-done.2, bf16[4,144,256]{2,1,0:T(8,128)(2,1)S(1)} %get-tuple-element.8.main_ref, bf16[4,16,256]{2,1,0:T(8,128)(2,1)S(1)} %get-tuple-element.9.edge_ref), custom_call_target="tpu_custom_call" | custom-call | flops 1048576 | bytes 2097152 | tf_op jit(solution)/shard_map/exchange/pallas_call | solution.py:319
  35.7 0.0 copy-done.1
  35.7 6.7 %backward.1 = bf16[32,128,256]{2,1,0:T(8,128)(2,1)} custom-call(f32[32,17]{1,0:T(8,128)S(1)} %pad_maximum_fusion.params_ref, s32[32,1]{1,0:T(8,128)S(1)} %copy.19.targets_ref, bf16[32,128,256]{2,1,0:T(8,128)(2,1)S(1)} %bitcast.13, bf16[4,144,256]{2,1,0:T(8,128)(2,1)S(1)} %get-tuple-element.12.low_ref), custom_call_target="tpu_custom_call" | custom-call | flops 1073741824 | bytes 5242880 | tf_op jit(solution)/shard_map/backward/pallas_call | solution.py:346
  42.4 0.7 %copy.23 = f32[1,1,128,256]{3,2,1,0:T(8,128)} copy(f32[1,1,128,256]{3,2,1,0:T(8,128)S(1)} %bitcast.14) | data formatting | bytes 262144
  43.1 0.6 %copy.24 = f32[1,64,256]{2,1,0:T(8,128)} copy(f32[1,64,256]{2,1,0:T(8,128)S(1)} %bitcast.15) | data formatting | bytes 131072
  (1 shorter events, 0.0 us)
Async XLA Ops:
  3.8 1.6 %copy-start = (bf16[1,1,32,128,256]{4,3,2,1,0:T(8,128)(2,1)S(1)}, bf16[1,1,32,128,256]{4,3,2,1,0:T(8,128)(2,1)}, u32[]{:S(2)}) copy-start(bf16[1,1,32,128,256]{4,3,2,1,0:T(8,128)(2,1)} %param.7) | copy-start | bytes 6291460
  5.4 7.7 %copy-start.2 = (f32[2]{0:T(128)S(1)}, f32[2]{0:T(128)}, u32[]{:S(2)}) copy-start(f32[2]{0:T(128)} %gain_ref.1) | copy-start | bytes 28
  5.4 30.3 %copy-start.1 = (bf16[1,1,32,128,256]{4,3,2,1,0:T(8,128)(2,1)S(1)}, bf16[1,1,32,128,256]{4,3,2,1,0:T(8,128)(2,1)}, u32[]{:S(2)}) copy-start(bf16[1,1,32,128,256]{4,3,2,1,0:T(8,128)(2,1)} %param.7) | copy-start | bytes 6291460

commit v2 on v1

v2 whole, which is shorter than its diff:
```python
import functools
import math

import jax
import jax.numpy as jnp
from jax import lax
from jax.experimental import pallas as pl
from jax.experimental.pallas import tpu as pltpu
from jax.sharding import PartitionSpec as P

EDGE = 16
MESH = pl.DeviceIdType.MESH


def lanczos(x):
    w = (x * x) * jnp.float32((math.pi / 3.0) ** 2)
    q = jnp.full_like(w, (-1.0) ** 10 / math.factorial(21))
    for k in range(9, -1, -1):
        q = q * w + jnp.float32((-1.0) ** k / math.factorial(2 * k + 1))
    q2 = q * q
    value = q2 * (1.0 - jnp.float32(4.0 / 3.0) * w * q2)
    return jnp.where(jnp.abs(x) < 3.0, value, 0.0)


def skewed(shift, taps):
    row = lax.broadcasted_iota(jnp.int32, (8, 128), 0)
    lane = lax.broadcasted_iota(jnp.int32, (8, 128), 1)
    lag = (lane - 64 - row).astype(jnp.float32)
    table = lanczos(lag - shift)
    mid = top = bottom = None
    for d in range(-3, 4):
        term = taps(d + 3) * (table if d == 0 else pltpu.roll(table, d % 128, 1))
        term_top = term if d >= 0 else jnp.where(row + d >= 0, term, 0.0)
        term_bottom = term if d <= 0 else jnp.where(row + d < 8, term, 0.0)
        mid = term if mid is None else mid + term
        top = term_top if top is None else top + term_top
        bottom = term_bottom if bottom is None else bottom + term_bottom
    return top, mid, bottom


def place(block, k):
    amount = (8 * k - 64) % 128
    return block if amount == 0 else pltpu.roll(block, amount, 1)


def low_half(block):
    lane = lax.broadcasted_iota(jnp.int32, block.shape, 1)
    return jnp.where(lane < 64, block, 0.0)


def high_half(block):
    lane = lax.broadcasted_iota(jnp.int32, block.shape, 1)
    return jnp.where(lane >= 64, block, 0.0)


def pair(first, second):
    return jnp.concatenate([first, second], axis=0).astype(jnp.bfloat16)


def build_columns(params_ref, t, put):
    top, mid, bottom = skewed(params_ref[t, 0], lambda d: params_ref[t, 2 + d])
    rolled = [place(mid, k) for k in range(16)]
    blocks = rolled + rolled
    blocks[0], blocks[31] = place(top, 0), place(bottom, 31)
    zero = jnp.zeros((16, 128), jnp.bfloat16)
    for q in range(16):
        both = blocks[2 * q], blocks[2 * q + 1]
        if q > 8:
            put(q, 0, zero)
        elif q in (7, 8):
            put(q, 0, pair(*[high_half(b) for b in both]))
        else:
            put(q, 0, pair(*[low_half(b) if q == 0 else b for b in both]))
        if q < 7:
            put(q, 1, zero)
        elif q in (7, 8):
            put(q, 1, pair(*[low_half(b) for b in both]))
        else:
            put(q, 1, pair(*[high_half(b) if q == 15 else b for b in both]))


def build_rows(params_ref, t, side, scale, put):
    top, mid, bottom = skewed(params_ref[t, 1], lambda d: params_ref[t, 9 + d])
    top, mid, bottom = top * scale, mid * scale, bottom * scale
    upper = side == 0
    first = jnp.where(upper, top, mid)
    last = jnp.where(upper, mid, bottom)
    blocks = [place(first, 0)] + [place(mid, k) for k in range(1, 15)] + [place(last, 15)]
    for q in range(8):
        both = blocks[2 * q], blocks[2 * q + 1]
        if q == 0:
            both = [low_half(b) for b in both]
        if q == 7:
            both = [high_half(b) for b in both]
        put(q, pair(*both))
    below = [high_half(place(mid, 16 + h)) for h in range(2)]
    above = [low_half(place(mid, h - 2)) for h in range(2)]
    put(8, pair(*[jnp.where(upper, b, a) for b, a in zip(below, above)]))


def coadd_kernel(
    patches, bands, group, params_ref, targets_ref, gain_ref, tiles_hbm,
    coadd_ref, detection_ref, out_hbm,
    tiles_ref, diff_ref, cols_ref, rows_ref, turned_ref, section_ref, mask_ref, den_ref,
    near_out, edge_out, far_out, near_in, edge_in, far_in, low_ref, gained_out, gained_in,
    tile_sem, out_sem, near_send, near_recv, edge_send, edge_recv, far_send, far_recv,
    near_back_send, near_back_recv, edge_back_send, edge_back_recv, far_back_send, far_back_recv,
    band_send, band_recv,
):
    me = lax.axis_index("patch")
    band = lax.axis_index("band")
    side = lax.axis_index("row")
    holding, height = tiles_ref.shape[:2]
    share = detection_ref.shape[0]
    half = height // 2
    groups = holding // group
    across = 1 - side
    near_at = pl.multiple_of((1 - side) * half, EDGE)
    far_at = pl.multiple_of(side * half, EDGE)
    edge_at = pl.multiple_of((1 - side) * (half - EDGE), EDGE)

    def tile_copy(i):
        part = pl.ds(i * group, group)
        return pltpu.make_async_copy(tiles_hbm.at[part], tiles_ref.at[part], tile_sem.at[i])

    def out_copy(i):
        part = pl.ds(i * group, group)
        return pltpu.make_async_copy(diff_ref.at[part], out_hbm.at[part], out_sem.at[i])

    for i in range(groups):
        tile_copy(i).start()
    barrier = pltpu.get_barrier_semaphore()
    for k in range(1, patches):
        z = lax.rem(me + k, patches)
        pl.semaphore_signal(barrier, inc=1, device_id={"patch": z}, device_id_type=MESH)
    for k in range(patches):
        z = lax.rem(me + k, patches)
        pl.semaphore_signal(
            barrier, inc=1, device_id={"patch": z, "row": across}, device_id_type=MESH
        )
    for k in range(1, bands):
        b = lax.rem(band + k, bands)
        pl.semaphore_signal(barrier, inc=1, device_id={"band": b}, device_id_type=MESH)

    def remote(source, place_at, send, recv, where):
        return pltpu.make_async_remote_copy(
            src_ref=source, dst_ref=place_at, send_sem=send, recv_sem=recv,
            device_id=where, device_id_type=MESH,
        )

    den_ref[...] = jnp.zeros_like(den_ref)
    index = lax.broadcasted_iota(jnp.int32, den_ref.shape, 0)

    @pl.loop(0, groups)
    def _(i):
        tile_copy(i).wait()
        for g in range(group):
            t = i * group + g
            weight = params_ref[t, 16]
            lanes = pl.ds(pl.multiple_of(t * 128, 128), 128)

            def put_col(q, part, tile):
                cols_ref[t, 16 * q : 16 * q + 16, 128 * part : 128 * part + 128] = tile

            def put_row(q, tile):
                if q == 8:
                    start = half
                elif q < 4:
                    start = 16 * q + (1 - side) * (half + EDGE)
                else:
                    start = 16 * (q - 4) + side * (half + EDGE)
                rows_ref[pl.ds(pl.multiple_of(start, EDGE), EDGE), lanes] = tile

            build_columns(params_ref, t, put_col)
            build_rows(params_ref, t, side, weight, put_row)
            section = lax.dot_general(
                tiles_ref[t], cols_ref[t], (((1,), (1,)), ((), ())), preferred_element_type=jnp.float32
            )
            section_ref[pl.ds(pl.multiple_of(t * height, height), height), :] = section.astype(jnp.bfloat16)
            chosen = index == targets_ref[t, 0]
            mask_ref[:, lanes] = jnp.where(chosen, 1.0, 0.0)
            den_ref[...] += jnp.where(chosen, weight, 0.0)

    pl.semaphore_wait(barrier, 2 * patches - 1 + bands - 1)

    def near_copy(k):
        z = lax.rem(me + k, patches)
        return remote(near_out.at[k], near_in.at[k], near_send.at[k], near_recv.at[k], {"patch": z})

    def edge_copy(k):
        z = lax.rem(me + k, patches)
        return remote(
            edge_out.at[k], edge_in.at[k], edge_send.at[k], edge_recv.at[k], {"patch": z, "row": across}
        )

    def far_copy(k):
        z = lax.rem(me + k, patches)
        return remote(far_out.at[k], far_in.at[k], far_send.at[k], far_recv.at[k], {"patch": z})

    def patch_sum(z, start, size):
        mask = mask_ref[pl.ds(z, 1), :].astype(jnp.bfloat16)
        return jnp.dot(
            rows_ref[start : start + size] * mask, section_ref[...], preferred_element_type=jnp.float32
        ).astype(jnp.bfloat16)

    def near_sum(k):
        z = lax.rem(me + k, patches)
        total = patch_sum(z, 0, half + EDGE)
        near_out[k, :half] = total[:half]
        edge_out[k] = total[half:]
        den = den_ref[pl.ds(z, 1), :]
        den = jnp.concatenate([den, den], axis=1)
        high = den.astype(jnp.bfloat16).astype(jnp.float32)
        line = lax.broadcasted_iota(jnp.int32, (EDGE, 256), 0)
        parts = jnp.where(line == 0, high, jnp.where(line == 1, den - high, 0.0))
        near_out[k, half:] = parts.astype(jnp.bfloat16)

    @pl.loop(1, patches)
    def _(k):
        near_sum(k)
        near_copy(k).start()
        edge_copy(k).start()

    near_sum(0)
    edge_copy(0).start()

    @pl.loop(1, patches)
    def _(k):
        far_out[k] = patch_sum(lax.rem(me + k, patches), half + EDGE, half)
        far_copy(k).start()

    far_out[0] = patch_sum(me, half + EDGE, half)

    def turn(t):
        lanes = pl.ds(pl.multiple_of(t * 128, 128), 128)
        block = rows_ref[:, lanes].astype(jnp.float32) * (1.0 / params_ref[t, 16])
        turned_ref[t] = block.T.astype(jnp.bfloat16)

    @pl.loop(0, holding // 8)
    def _(i):
        for g in range(4):
            turn(i * 4 + g)

    for k in range(1, patches):
        near_copy(k).wait()
    for k in range(patches):
        edge_copy(k).wait()
    total = near_out[0].astype(jnp.float32)
    beside = edge_in[0].astype(jnp.float32)
    for k in range(1, patches):
        total += near_in[k].astype(jnp.float32)
        beside += edge_in[k].astype(jnp.float32)
    factor = 1.0 / (1.0 + jnp.sum(total[half:], axis=0, keepdims=True))
    zero = jnp.zeros((half - EDGE, 256), jnp.float32)
    beside = jnp.where(
        side == 0,
        jnp.concatenate([zero, beside], axis=0),
        jnp.concatenate([beside, zero], axis=0),
    )
    near = (total[:half] + beside) * factor
    low_ref[me, :half] = near.astype(jnp.bfloat16)

    def near_back(k):
        z = lax.rem(me + k, patches)
        here = low_ref.at[me, pl.ds(0, half)]
        return remote(here, here, near_back_send.at[k], near_back_recv.at[k], {"patch": z})

    def edge_back(k):
        z = lax.rem(me + k, patches)
        return remote(
            low_ref.at[me, pl.ds(edge_at, EDGE)], low_ref.at[me, pl.ds(half, EDGE)],
            edge_back_send.at[k], edge_back_recv.at[k], {"patch": z, "row": across},
        )

    def far_back(k):
        z = lax.rem(me + k, patches)
        here = low_ref.at[me, pl.ds(half + EDGE, half)]
        return remote(here, here, far_back_send.at[k], far_back_recv.at[k], {"patch": z})

    for k in range(1, patches):
        near_back(k).start()
    for k in range(patches):
        edge_back(k).start()
    coadd_ref[pl.ds(near_at, half), :] = near
    gained_out[pl.ds(near_at, half), :] = (gain_ref[band] * near).astype(jnp.bfloat16)

    for k in range(1, patches):
        far_copy(k).wait()
    far = far_out[0].astype(jnp.float32)
    for k in range(1, patches):
        far += far_in[k].astype(jnp.float32)
    far = far * factor
    low_ref[me, half + EDGE :] = far.astype(jnp.bfloat16)
    for k in range(1, patches):
        far_back(k).start()
    coadd_ref[pl.ds(far_at, half), :] = far
    gained_out[pl.ds(far_at, half), :] = (gain_ref[band] * far).astype(jnp.bfloat16)

    def band_copy(k):
        b = lax.rem(band + k, bands)
        return remote(
            gained_out.at[pl.ds(pl.multiple_of(b * share, EDGE), share)], gained_in.at[k],
            band_send.at[k], band_recv.at[k], {"band": b},
        )

    for k in range(1, bands):
        band_copy(k).start()

    @pl.loop(holding // 8, holding // 4)
    def _(i):
        for g in range(4):
            turn(i * 4 + g)

    for k in range(1, bands):
        band_copy(k).wait()
    detection = gain_ref[band] * coadd_ref[pl.ds(pl.multiple_of(band * share, EDGE), share), :]
    for k in range(1, bands):
        detection += gained_in[k].astype(jnp.float32)
    detection_ref[...] = detection

    for k in range(1, patches):
        near_back(k).wait()
    for k in range(patches):
        edge_back(k).wait()
    for k in range(1, patches):
        far_back(k).wait()

    @pl.loop(0, groups)
    def _(i):
        for g in range(group):
            t = i * group + g
            back = jnp.dot(
                turned_ref[t], low_ref[targets_ref[t, 0]], preferred_element_type=jnp.float32
            ).astype(jnp.bfloat16)
            template = jnp.dot(back, cols_ref[t], preferred_element_type=jnp.float32)
            template = template.astype(jnp.bfloat16).astype(jnp.float32)
            diff_ref[t] = (tiles_ref[t].astype(jnp.float32) - template).astype(jnp.bfloat16)
        out_copy(i).start()

    for i in range(groups):
        out_copy(i).wait()


def body(tiles, targets, offsets, fractions, kernels, weights, band_gain):
    holding, height, extent = tiles.shape[2:]
    patches, bands = lax.axis_size("patch"), lax.axis_size("band")
    images, target = tiles[0, 0], targets[0, 0]
    params = jnp.concatenate(
        [
            offsets[0, 0].astype(jnp.float32) + fractions[0, 0].astype(jnp.float32),
            kernels[0, 0].reshape(holding, 14).astype(jnp.float32),
            weights[0, 0][:, None].astype(jnp.float32),
        ],
        axis=1,
    )
    smem = pl.BlockSpec(memory_space=pltpu.SMEM)
    vmem = pl.BlockSpec(memory_space=pltpu.VMEM)
    anywhere = pl.BlockSpec(memory_space=pl.ANY)
    stored = pl.BlockSpec(memory_space=pltpu.HBM)
    group = 8
    padded = -(-patches // 8) * 8
    macs = holding * height * extent * extent
    share, half = height // bands, height // 2
    low, dma = jnp.bfloat16, pltpu.SemaphoreType.DMA
    per_patch = lambda rows: pltpu.VMEM((patches, rows, extent), low)
    coadd, detection, difference = pl.pallas_call(
        functools.partial(coadd_kernel, patches, bands, group),
        in_specs=[smem, smem, smem, stored],
        out_specs=[vmem, vmem, anywhere],
        out_shape=[
            jax.ShapeDtypeStruct((height, extent), jnp.float32),
            jax.ShapeDtypeStruct((share, extent), jnp.float32),
            jax.ShapeDtypeStruct((holding, height, extent), low),
        ],
        scratch_shapes=[
            pltpu.VMEM((holding, height, extent), low),
            pltpu.VMEM((holding, height, extent), low),
            pltpu.VMEM((holding, extent, extent), low),
            pltpu.VMEM((height + EDGE, holding * 128), low),
            pltpu.VMEM((holding, height, height + EDGE), low),
            pltpu.VMEM((holding * height, extent), low),
            pltpu.VMEM((padded, holding * 128), jnp.float32),
            pltpu.VMEM((padded, 128), jnp.float32),
            per_patch(half + EDGE),
            per_patch(EDGE),
            per_patch(half),
            per_patch(half + EDGE),
            per_patch(EDGE),
            per_patch(half),
            per_patch(height + EDGE),
            pltpu.VMEM((height, extent), low),
            pltpu.VMEM((bands, share, extent), low),
            dma((holding // group,)),
            dma((holding // group,)),
        ]
        + [dma((patches,))] * 12
        + [dma((bands,))] * 2,
        compiler_params=pltpu.CompilerParams(
            collective_id=0, has_side_effects=True, vmem_limit_bytes=48 << 20
        ),
        cost_estimate=pl.CostEstimate(flops=8 * macs, bytes_accessed=5 << 20, transcendentals=0),
        name="coadd",
    )(params, target, band_gain, images)
    return (coadd[None, None], detection[None], difference[None, None])


def solution(mesh):
    placed = (
        P(("tract", "band"), "patch", None, "row", None),
        P(("tract", "band"), "patch", None, None),
        P(("tract", "band"), "patch", None, None),
        P(("tract", "band"), "patch", None, None),
        P(("tract", "band"), "patch", None, None, None),
        P(("tract", "band"), "patch", None),
        P(),
    )
    return jax.shard_map(
        body,
        mesh=mesh,
        in_specs=placed,
        out_specs=(
            P(("tract", "band"), "patch", "row", None),
            P(("tract", "patch"), ("row", "band"), None),
            P(("tract", "band"), "patch", None, "row", None),
        ),
        check_vma=False,
    )
```

time: 43.9 us -> 36 us (0.82)
  Pallas kernels: 37 us -> 27.1 us
  local copies, waits for them, and re-layouts: 4.57 us -> 6.54 us
    pallas_call x3 -> x1, Pallas kernels: 37 us -> 27.1 us  [body(): pl.pallas_call(functools.partial(coadd_kernel, patches, bands, group), in...]
    unnamed x8 -> x7, local copies, waits for them, and re-layouts: 2.88 us -> 4.85 us
where the time goes in v2:
time: 36 us; the launch traced here: 35.7 us
  Pallas kernels  27.1 us (75%)
  local copies, waits for them, and re-layouts  6.54 us (18%)
  other arithmetic  1.43 us (4%)
  between operations  0.65 us (2%)
    pallas_call x1, Pallas kernels, body(): pl.pallas_call(functools.partial(coadd_kernel, patches, bands, group), in...  27.1 us
    unnamed x7, local copies, waits for them, and re-layouts  4.85 us
    convert_element_type x3, local copies, waits for them, and re-layouts, body(): kernels[0, 0].reshape(holding, 14).astype(jnp.float32)  0.78 us
    squeeze x1, local copies, waits for them, and re-layouts, body(): images, target = (tiles[0, 0], targets[0, 0])  0.74 us

profile of v2, /device:TPU:0, one launch (start us, length us, event | category | flops | bytes accessed | tf_op | source)
XLA Modules:
  0.0 35.7 jit_solution(8885508564252104599)
XLA Ops:
  0.6 0.7 %bitcast_convert_fusion = f32[32,1]{0,1:T(1,128)S(1)} fusion(bf16[1,1,32]{2,1,0:T(2,128)(2,1)} %param.12), kind=kLoop, calls=%fused_computation.2 | loop fusion | flops 32 | bytes 192 | tf_op jit(solution)/shard_map/convert_element_type | solution.py:352
  1.3 0.7 %add_bitcast_fusion = f32[32,2]{0,1:T(2,128)S(1)} fusion(bf16[1,1,32,2]{2,3,1,0:T(2,128)(2,1)} %param.10, s32[1,1,32,2]{2,3,1,0:T(2,128)} %param.9), kind=kLoop, calls=%fused_computation.1 | loop fusion | flops 192 | bytes 640 | tf_op jit(solution)/shard_map/add | solution.py:350
  2.0 0.7 %copy.14 = f32[1,1,32,2,7]{2,4,3,1,0:T(8,128)S(1)} copy(bf16[1,1,32,2,7]{2,3,4,1,0:T(2,128)(2,1)} %param.11) | data formatting | bytes 2688 | tf_op jit(solution)/shard_map/convert_element_type | solution.py:351
  2.7 0.1 copy.16
  2.8 0.1 copy.15
  2.9 0.1 copy.17
  2.9 0.1 pad_maximum_fusion.params_ref
  3.0 0.7 %copy.18.targets_ref = s32[32,1]{1,0:T(8,128)S(1)} copy(s32[32,1]{0,1:T(1,128)} %bitcast.16) | data formatting | bytes 256 | tf_op jit(solution)/shard_map/squeeze | solution.py:347
  3.8 0.0 copy-start
  3.8 1.6 %copy-done = bf16[1,1,32,128,256]{4,3,2,1,0:T(8,128)(2,1)S(1)} copy-done((bf16[1,1,32,128,256]{4,3,2,1,0:T(8,128)(2,1)S(1)}, bf16[1,1,32,128,256]{4,3,2,1,0:T(8,128)(2,1)}, u32[]{:S(2)}) %copy-start) | copy-done | bytes 2097176
  5.4 0.0 copy-start.1
  5.4 0.7 %copy-done.1 = f32[2]{0:T(128)S(1)} copy-done((f32[2]{0:T(128)S(1)}, f32[2]{0:T(128)}, u32[]{:S(2)}) %copy-start.1) | copy-done | bytes 32
  6.0 27.1 %coadd.1 = (f32[128,256]{1,0:T(8,128)S(1)}, f32[64,256]{1,0:T(8,128)S(1)}, bf16[32,128,256]{2,1,0:T(8,128)(2,1)S(1)}) custom-call(f32[32,17]{1,0:T(8,128)S(1)} %pad_maximum_fusion.params_ref, s32[32,1]{1,0:T(8,128)S(1)} %copy.18.targets_ref, f32[2]{0:T(128)S(1)} %copy-done.1, bf16[32,128,256]{2,1,0:T(8,128)(2,1)S(1)} %bitcast.15), custom_call_target="tpu_custom_call" | custom-call | flops 2147483648 | bytes 5242880 | tf_op jit(solution)/shard_map/coadd/pallas_call | solution.py:366
  33.1 0.7 %copy.22 = f32[1,1,128,256]{3,2,1,0:T(8,128)} copy(f32[1,1,128,256]{3,2,1,0:T(8,128)S(1)} %bitcast.13) | data formatting | bytes 262144
  33.8 0.6 %copy.23 = f32[1,64,256]{2,1,0:T(8,128)} copy(f32[1,64,256]{2,1,0:T(8,128)S(1)} %bitcast.14) | data formatting | bytes 131072
  34.4 1.3 %copy.24 = bf16[1,1,32,128,256]{4,3,2,1,0:T(8,128)(2,1)} copy(bf16[1,1,32,128,256]{4,3,2,1,0:T(8,128)(2,1)S(1)} %bitcast.12) | data formatting | bytes 4194304
  (1 shorter events, 0.0 us)
Async XLA Ops:
  3.8 1.6 %copy-start = (bf16[1,1,32,128,256]{4,3,2,1,0:T(8,128)(2,1)S(1)}, bf16[1,1,32,128,256]{4,3,2,1,0:T(8,128)(2,1)}, u32[]{:S(2)}) copy-start(bf16[1,1,32,128,256]{4,3,2,1,0:T(8,128)(2,1)} %param.7) | copy-start | bytes 6291460
  5.4 0.7 %copy-start.1 = (f32[2]{0:T(128)S(1)}, f32[2]{0:T(128)}, u32[]{:S(2)}) copy-start(f32[2]{0:T(128)} %gain_ref.1) | copy-start | bytes 28

commit v3 on v2

--- a/solution.py
+++ b/solution.py
@@ -58,7 +58,7 @@
 
 
 def build_columns(params_ref, t, put):
-    top, mid, bottom = skewed(params_ref[t, 0], lambda d: params_ref[t, 2 + d])
+    top, mid, bottom = skewed(params_ref[0, t], lambda d: params_ref[2 + 2 * d, t])
     rolled = [place(mid, k) for k in range(16)]
     blocks = rolled + rolled
     blocks[0], blocks[31] = place(top, 0), place(bottom, 31)
@@ -80,7 +80,7 @@
 
 
 def build_rows(params_ref, t, side, scale, put):
-    top, mid, bottom = skewed(params_ref[t, 1], lambda d: params_ref[t, 9 + d])
+    top, mid, bottom = skewed(params_ref[1, t], lambda d: params_ref[3 + 2 * d, t])
     top, mid, bottom = top * scale, mid * scale, bottom * scale
     upper = side == 0
     first = jnp.where(upper, top, mid)
@@ -99,11 +99,12 @@
 
 
 def coadd_kernel(
-    patches, bands, group, params_ref, targets_ref, gain_ref, tiles_hbm,
-    coadd_ref, detection_ref, out_hbm,
-    tiles_ref, diff_ref, cols_ref, rows_ref, turned_ref, section_ref, mask_ref, den_ref,
-    near_out, edge_out, far_out, near_in, edge_in, far_in, low_ref, gained_out, gained_in,
-    tile_sem, out_sem, near_send, near_recv, edge_send, edge_recv, far_send, far_recv,
+    patches, bands, group, offsets_ref, fractions_ref, kernels_ref, weights_ref, targets_ref, gain_ref,
+    tiles_hbm,
+    coadd_ref, detection_ref, low_ref, cols_hbm, turned_hbm,
+    staged_ref, params_ref, params_sem, cols_ref, turned_ref, cols_sem, turned_sem, tiles_ref, rows_ref, section_ref, mask_ref, den_ref,
+    near_out, edge_out, far_out, near_in, edge_in, far_in, gained_out, gained_in,
+    tile_sem, near_send, near_recv, edge_send, edge_recv, far_send, far_recv,
     near_back_send, near_back_recv, edge_back_send, edge_back_recv, far_back_send, far_back_recv,
     band_send, band_recv,
 ):
@@ -123,12 +124,15 @@
         part = pl.ds(i * group, group)
         return pltpu.make_async_copy(tiles_hbm.at[part], tiles_ref.at[part], tile_sem.at[i])
 
-    def out_copy(i):
-        part = pl.ds(i * group, group)
-        return pltpu.make_async_copy(diff_ref.at[part], out_hbm.at[part], out_sem.at[i])
-
     for i in range(groups):
         tile_copy(i).start()
+    staged_ref[...] = jnp.zeros_like(staged_ref)
+    staged_ref[0:2, :holding] = offsets_ref[...].astype(jnp.float32) + fractions_ref[...].astype(jnp.float32)
+    for d in range(7):
+        staged_ref[2 + 2 * d : 4 + 2 * d, :holding] = kernels_ref[d].astype(jnp.float32)
+    staged_ref[16:17, :holding] = weights_ref[...].astype(jnp.float32)
+    params_copy = pltpu.make_async_copy(staged_ref, params_ref, params_sem)
+    params_copy.start()
     barrier = pltpu.get_barrier_semaphore()
     for k in range(1, patches):
         z = lax.rem(me + k, patches)
@@ -148,6 +152,7 @@
             device_id=where, device_id_type=MESH,
         )
 
+    params_copy.wait()
     den_ref[...] = jnp.zeros_like(den_ref)
     index = lax.broadcasted_iota(jnp.int32, den_ref.shape, 0)
 
@@ -156,7 +161,7 @@
         tile_copy(i).wait()
         for g in range(group):
             t = i * group + g
-            weight = params_ref[t, 16]
+            weight = params_ref[16, t]
             lanes = pl.ds(pl.multiple_of(t * 128, 128), 128)
 
             def put_col(q, part, tile):
@@ -177,10 +182,12 @@
                 tiles_ref[t], cols_ref[t], (((1,), (1,)), ((), ())), preferred_element_type=jnp.float32
             )
             section_ref[pl.ds(pl.multiple_of(t * height, height), height), :] = section.astype(jnp.bfloat16)
-            chosen = index == targets_ref[t, 0]
+            chosen = index == targets_ref[0, t]
             mask_ref[:, lanes] = jnp.where(chosen, 1.0, 0.0)
             den_ref[...] += jnp.where(chosen, weight, 0.0)
 
+    cols_copy = pltpu.make_async_copy(cols_ref, cols_hbm, cols_sem)
+    turned_copy = pltpu.make_async_copy(turned_ref, turned_hbm, turned_sem)
     pl.semaphore_wait(barrier, 2 * patches - 1 + bands - 1)
 
     def near_copy(k):
@@ -197,43 +204,50 @@
         z = lax.rem(me + k, patches)
         return remote(far_out.at[k], far_in.at[k], far_send.at[k], far_recv.at[k], {"patch": z})
 
-    def patch_sum(z, start, size):
-        mask = mask_ref[pl.ds(z, 1), :].astype(jnp.bfloat16)
-        return jnp.dot(
-            rows_ref[start : start + size] * mask, section_ref[...], preferred_element_type=jnp.float32
+    block = next(n for n in (4, 2, 1) if patches % n == 0)
+
+    def patch_sums(first, start, size):
+        rows = rows_ref[start : start + size]
+        masked = []
+        for j in range(block):
+            z = lax.rem(me + first + j, patches)
+            masked.append(rows * mask_ref[pl.ds(z, 1), :].astype(jnp.bfloat16))
+        total = jnp.dot(
+            jnp.concatenate(masked, axis=0), section_ref[...], preferred_element_type=jnp.float32
         ).astype(jnp.bfloat16)
-
-    def near_sum(k):
-        z = lax.rem(me + k, patches)
-        total = patch_sum(z, 0, half + EDGE)
-        near_out[k, :half] = total[:half]
-        edge_out[k] = total[half:]
-        den = den_ref[pl.ds(z, 1), :]
-        den = jnp.concatenate([den, den], axis=1)
-        high = den.astype(jnp.bfloat16).astype(jnp.float32)
-        line = lax.broadcasted_iota(jnp.int32, (EDGE, 256), 0)
-        parts = jnp.where(line == 0, high, jnp.where(line == 1, den - high, 0.0))
-        near_out[k, half:] = parts.astype(jnp.bfloat16)
-
-    @pl.loop(1, patches)
-    def _(k):
-        near_sum(k)
+        return [total[size * j : size * j + size] for j in range(block)]
+
+    @pl.loop(0, patches // block)
+    def _(i):
+        for j, total in enumerate(patch_sums(i * block, 0, half + EDGE)):
+            k = i * block + j
+            near_out[k, :half] = total[:half]
+            edge_out[k] = total[half:]
+            den = den_ref[pl.ds(lax.rem(me + k, patches), 1), :]
+            den = jnp.concatenate([den, den], axis=1)
+            high = den.astype(jnp.bfloat16).astype(jnp.float32)
+            line = lax.broadcasted_iota(jnp.int32, (EDGE, 256), 0)
+            parts = jnp.where(line == 0, high, jnp.where(line == 1, den - high, 0.0))
+            near_out[k, half:] = parts.astype(jnp.bfloat16)
+
+    for k in range(1, patches):
         near_copy(k).start()
+    for k in range(patches):
         edge_copy(k).start()
 
-    near_sum(0)
-    edge_copy(0).start()
-
-    @pl.loop(1, patches)
-    def _(k):
-        far_out[k] = patch_sum(lax.rem(me + k, patches), half + EDGE, half)
+    @pl.loop(0, patches // block)
+    def _(i):
+        for j, total in enumerate(patch_sums(i * block, half + EDGE, half)):
+            far_out[i * block + j] = total
+
+    for k in range(1, patches):
         far_copy(k).start()
 
-    far_out[0] = patch_sum(me, half + EDGE, half)
+    cols_copy.start()
 
     def turn(t):
         lanes = pl.ds(pl.multiple_of(t * 128, 128), 128)
-        block = rows_ref[:, lanes].astype(jnp.float32) * (1.0 / params_ref[t, 16])
+        block = rows_ref[:, lanes].astype(jnp.float32) * (1.0 / params_ref[16, t])
         turned_ref[t] = block.T.astype(jnp.bfloat16)
 
     @pl.loop(0, holding // 8)
@@ -311,6 +325,7 @@
         for g in range(4):
             turn(i * 4 + g)
 
+    turned_copy.start()
     for k in range(1, bands):
         band_copy(k).wait()
     detection = gain_ref[band] * coadd_ref[pl.ds(pl.multiple_of(band * share, EDGE), share), :]
@@ -324,13 +339,45 @@
         edge_back(k).wait()
     for k in range(1, patches):
         far_back(k).wait()
+    cols_copy.wait()
+    turned_copy.wait()
+
+
+def template_kernel(
+    group, targets_ref, tiles_hbm, low_ref, cols_hbm, turned_hbm, coadd_ref, detection_ref,
+    coadd_out, detection_out, out_hbm, tiles_ref, cols_ref, turned_ref, diff_ref,
+    coadd_sem, detection_sem, out_sem, tile_sem, cols_sem, turned_sem,
+):
+    groups = tiles_ref.shape[0] // group
+
+    def out_copy(i):
+        part = pl.ds(i * group, group)
+        return pltpu.make_async_copy(diff_ref.at[part], out_hbm.at[part], out_sem.at[i])
+
+    def in_copies(i):
+        part = pl.ds(i * group, group)
+        return (
+            pltpu.make_async_copy(turned_hbm.at[part], turned_ref.at[part], turned_sem.at[i]),
+            pltpu.make_async_copy(cols_hbm.at[part], cols_ref.at[part], cols_sem.at[i]),
+            pltpu.make_async_copy(tiles_hbm.at[part], tiles_ref.at[part], tile_sem.at[i]),
+        )
+
+    for i in range(groups):
+        for copy in in_copies(i):
+            copy.start()
+    coadd_copy = pltpu.make_async_copy(coadd_ref, coadd_out, coadd_sem)
+    detection_copy = pltpu.make_async_copy(detection_ref, detection_out, detection_sem)
+    coadd_copy.start()
+    detection_copy.start()
 
     @pl.loop(0, groups)
     def _(i):
+        for copy in in_copies(i):
+            copy.wait()
         for g in range(group):
             t = i * group + g
             back = jnp.dot(
-                turned_ref[t], low_ref[targets_ref[t, 0]], preferred_element_type=jnp.float32
+                turned_ref[t], low_ref[targets_ref[0, t]], preferred_element_type=jnp.float32
             ).astype(jnp.bfloat16)
             template = jnp.dot(back, cols_ref[t], preferred_element_type=jnp.float32)
             template = template.astype(jnp.bfloat16).astype(jnp.float32)
@@ -339,45 +386,44 @@
 
     for i in range(groups):
         out_copy(i).wait()
+    coadd_copy.wait()
+    detection_copy.wait()
 
 
 def body(tiles, targets, offsets, fractions, kernels, weights, band_gain):
     holding, height, extent = tiles.shape[2:]
     patches, bands = lax.axis_size("patch"), lax.axis_size("band")
-    images, target = tiles[0, 0], targets[0, 0]
-    params = jnp.concatenate(
-        [
-            offsets[0, 0].astype(jnp.float32) + fractions[0, 0].astype(jnp.float32),
-            kernels[0, 0].reshape(holding, 14).astype(jnp.float32),
-            weights[0, 0][:, None].astype(jnp.float32),
-        ],
-        axis=1,
-    )
+    images, target = tiles[0, 0], targets[0, 0, :, 0][None, :]
     smem = pl.BlockSpec(memory_space=pltpu.SMEM)
     vmem = pl.BlockSpec(memory_space=pltpu.VMEM)
     anywhere = pl.BlockSpec(memory_space=pl.ANY)
-    stored = pl.BlockSpec(memory_space=pltpu.HBM)
     group = 8
     padded = -(-patches // 8) * 8
     macs = holding * height * extent * extent
     share, half = height // bands, height // 2
     low, dma = jnp.bfloat16, pltpu.SemaphoreType.DMA
     per_patch = lambda rows: pltpu.VMEM((patches, rows, extent), low)
-    coadd, detection, difference = pl.pallas_call(
+    coadd, detection, low_coadd, cols, turned = pl.pallas_call(
         functools.partial(coadd_kernel, patches, bands, group),
-        in_specs=[smem, smem, smem, stored],
-        out_specs=[vmem, vmem, anywhere],
+        in_specs=[vmem, vmem, vmem, vmem, smem, smem, anywhere],
+        out_specs=[vmem, vmem, vmem, anywhere, anywhere],
         out_shape=[
             jax.ShapeDtypeStruct((height, extent), jnp.float32),
             jax.ShapeDtypeStruct((share, extent), jnp.float32),
-            jax.ShapeDtypeStruct((holding, height, extent), low),
+            jax.ShapeDtypeStruct((patches, height + EDGE, extent), low),
+            jax.ShapeDtypeStruct((holding, extent, extent), low),
+            jax.ShapeDtypeStruct((holding, height, height + EDGE), low),
         ],
         scratch_shapes=[
+            pltpu.VMEM((24, 128), jnp.float32),
+            pltpu.SMEM((24, 128), jnp.float32),
+            dma,
+            pltpu.VMEM((holding, extent, extent), low),
+            pltpu.VMEM((holding, height, height + EDGE), low),
+            dma,
+            dma,
             pltpu.VMEM((holding, height, extent), low),
-            pltpu.VMEM((holding, height, extent), low),
-            pltpu.VMEM((holding, extent, extent), low),
             pltpu.VMEM((height + EDGE, holding * 128), low),
-            pltpu.VMEM((holding, height, height + EDGE), low),
             pltpu.VMEM((holding * height, extent), low),
             pltpu.VMEM((padded, holding * 128), jnp.float32),
             pltpu.VMEM((padded, 128), jnp.float32),
@@ -387,20 +433,48 @@
             per_patch(half + EDGE),
             per_patch(EDGE),
             per_patch(half),
-            per_patch(height + EDGE),
             pltpu.VMEM((height, extent), low),
             pltpu.VMEM((bands, share, extent), low),
-            dma((holding // group,)),
             dma((holding // group,)),
         ]
         + [dma((patches,))] * 12
         + [dma((bands,))] * 2,
         compiler_params=pltpu.CompilerParams(
-            collective_id=0, has_side_effects=True, vmem_limit_bytes=48 << 20
+            collective_id=0, has_side_effects=True, vmem_limit_bytes=60 << 20
         ),
-        cost_estimate=pl.CostEstimate(flops=8 * macs, bytes_accessed=5 << 20, transcendentals=0),
+        cost_estimate=pl.CostEstimate(flops=4 * macs, bytes_accessed=3 << 20, transcendentals=0),
         name="coadd",
-    )(params, target, band_gain, images)
+    )(
+        offsets[0, 0].T,
+        fractions[0, 0].T,
+        kernels[0, 0].transpose(2, 1, 0),
+        weights[0, 0][None, :],
+        target,
+        band_gain,
+        images,
+    )
+    coadd, detection, difference = pl.pallas_call(
+        functools.partial(template_kernel, group),
+        in_specs=[smem, anywhere, vmem, anywhere, anywhere, vmem, vmem],
+        out_specs=[anywhere, anywhere, anywhere],
+        out_shape=[
+            jax.ShapeDtypeStruct((height, extent), jnp.float32),
+            jax.ShapeDtypeStruct((share, extent), jnp.float32),
+            jax.ShapeDtypeStruct((holding, height, extent), low),
+        ],
+        scratch_shapes=[
+            pltpu.VMEM((holding, height, extent), low),
+            pltpu.VMEM((holding, extent, extent), low),
+            pltpu.VMEM((holding, height, height + EDGE), low),
+            pltpu.VMEM((holding, height, extent), low),
+            dma,
+            dma,
+        ]
+        + [dma((holding // group,))] * 4,
+        compiler_params=pltpu.CompilerParams(vmem_limit_bytes=60 << 20),
+        cost_estimate=pl.CostEstimate(flops=4 * macs, bytes_accessed=3 << 20, transcendentals=0),
+        name="templates",
+    )(target, images, low_coadd, cols, turned, coadd, detection)
     return (coadd[None, None], detection[None], difference[None, None])
 
 

time: 36 us -> 33.5 us (0.931)
  local copies, waits for them, and re-layouts: 6.54 us -> 0 us
  Pallas kernels: 27.1 us -> 32.7 us
  other arithmetic: 1.43 us -> 0 us
    pallas_call x0 -> x1, Pallas kernels: none -> 6.16 us  [body(): pl.pallas_call(functools.partial(template_kernel, group), in_specs=[smem,...]
    unnamed x7 -> x0, local copies, waits for them, and re-layouts: 4.85 us -> none
    convert_element_type x4 -> x0, local copies, waits for them, and re-layouts: 0.87 us -> none  [the longest x3 0.78 us: body(): kernels[0, 0].reshape(holding, 14).astype(jnp.float32)]
    squeeze x1 -> x0, local copies, waits for them, and re-layouts: 0.74 us -> none  [body(): images, target = (tiles[0, 0], targets[0, 0])]
    add x1 -> x0, other arithmetic: 0.7 us -> none  [body(): offsets[0, 0].astype(jnp.float32) + fractions[0, 0].astype(jnp.float32)]
    convert_element_type x1 -> x0, other arithmetic: 0.66 us -> none  [body(): weights[0, 0][:, None].astype(jnp.float32)]
    pallas_call x1, Pallas kernels: 27.1 us -> 26.5 us  [body(): pl.pallas_call(functools.partial(coadd_kernel, patches, bands, group), in...]
where the time goes in v3:
time: 33.5 us; the launch traced here: 33.3 us
  Pallas kernels  32.7 us (98%)
  between operations  0.64 us (2%)
    pallas_call x1, Pallas kernels, body(): pl.pallas_call(functools.partial(coadd_kernel, patches, bands, group), in...  26.5 us
    pallas_call x1, Pallas kernels, body(): pl.pallas_call(functools.partial(template_kernel, group), in_specs=[smem,...  6.16 us

profile of v3, /device:TPU:0, one launch (start us, length us, event | category | flops | bytes accessed | tf_op | source)
XLA Modules:
  0.0 33.3 jit_solution(10372136038760271884)
XLA Ops:
  0.6 26.5 %coadd.1 = (f32[128,256]{1,0:T(8,128)}, f32[64,256]{1,0:T(8,128)}, bf16[4,144,256]{2,1,0:T(8,128)(2,1)}, bf16[32,256,256]{2,1,0:T(8,128)(2,1)}, bf16[32,128,144]{2,1,0:T(8,128)(2,1)}) custom-call(s32[2,32]{1,0:T(2,128)} %bitcast.23, bf16[2,32]{1,0:T(2,128)(2,1)} %bitcast.24, bf16[7,2,32]{2,1,0:T(2,128)(2,1)} %bitcast.22, bf16[1,32]{1,0:T(2,128)(2,1)} %bitcast.25, ...), custom_call_target="tpu_custom_call" | custom-call | flops 1073741824 | bytes 3145728 | tf_op jit(solution)/shard_map/coadd/pallas_call | solution.py:406
  27.2 6.2 %templates.1 = (f32[128,256]{1,0:T(8,128)}, f32[64,256]{1,0:T(8,128)}, bf16[32,128,256]{2,1,0:T(8,128)(2,1)}) custom-call(s32[1,32]{1,0:T(1,128)} %bitcast.18, bf16[32,128,256]{2,1,0:T(8,128)(2,1)} %bitcast.16, bf16[4,144,256]{2,1,0:T(8,128)(2,1)} %get-tuple-element.11.low_ref, bf16[32,256,256]{2,1,0:T(8,128)(2,1)} %get-tuple-element.12.cols_hbm, ...), custom_call_target="tpu_custom_call" | custom-call | flops 1073741824 | bytes 3145728 | tf_op jit(solution)/shard_map/templates/pallas_call | solution.py:456
